TPU v7x, 32 devices: a whole 2x2x4 slice. The times are simulated.
32 devices in a mesh: ctx: 8 (over z, x), ch: 4 (over y, core).
Axes of the slice: x: 2, y: 2, z: 4, core: 2. Of those that a mesh axis runs over, the one named last changes fastest.
Arguments:
- query_act: bfloat16 [1024, 4096], P('ctx', 'ch'), may hold values from -6 to 6
- key_act: bfloat16 [1024, 4096], P('ctx', 'ch'), may hold values from -6 to 6
- value_act: bfloat16 [1024, 4096], P('ctx', 'ch'), may hold values from -6 to 6
- filters: bfloat16 [256, 128], P('ch'), may hold values from -0.5 to 0.5
- skip_bias: float32 [4096], P('ch'), may hold values from -4 to 4
- out_weight: bfloat16 [4096, 8192], P('ch'), may hold values from -0.09375 to 0.09375
- out_grad: bfloat16 [1024, 8192], P('ctx', 'ch'), may hold values from -6 to 6
Outputs:
- gated: bfloat16 [1024, 4096], P('ctx', 'ch')
- query_grad: bfloat16 [1024, 4096], P('ctx', 'ch')
- key_grad: bfloat16 [1024, 4096], P('ctx', 'ch')
- value_grad: bfloat16 [1024, 4096], P('ctx', 'ch')
- filter_grad: float32 [256, 128], P('ch')
- skip_grad: float32 [4096], P('ch')
All inputs are finite; a program needn't handle non-finite values.
Results may differ from a plain program's by a relative error of at most 0.0075.
Values may be sent and summed in bfloat16 or wider, within the bound.
A program may use at most 64 MiB of HBM per device.

v0:
```python
import jax
import jax.numpy as jnp
from jax import lax
from jax.sharding import PartitionSpec as P


def passed_along(block, axis, distance):
    devices = range(lax.axis_size(axis))
    route = [(i - distance, i) for i in devices if i - distance in devices]
    return lax.ppermute(block, axis, route)


def toeplitz(first, tok_rows, span_width):
    group_count = first.shape[0]
    extended = jnp.concatenate([first, jnp.zeros((group_count, 1), first.dtype)], axis=1)
    tiled = jnp.tile(extended, (1, tok_rows))
    return tiled[:, : tok_rows * span_width].reshape(group_count, tok_rows, span_width)


def per_device(query_act, key_act, value_act, filters, skip_bias, out_weight, out_grad):
    tok_rows, chan_width = query_act.shape
    group_count, tap_count = filters.shape
    group_size = chan_width // group_count
    rim_len = tap_count - 1
    span_width = tok_rows + rim_len
    query_f = query_act.astype(jnp.float32)
    key_f = key_act.astype(jnp.float32)
    value_f = value_act.astype(jnp.float32)
    inner = (key_f * value_f).astype(jnp.bfloat16)
    mixed_grad = lax.dot_general(
        lax.all_gather(out_grad, "ch", axis=1, tiled=True),
        out_weight,
        (((1,), (1,)), ((), ())),
        preferred_element_type=jnp.float32,
    )
    conv_grad = (mixed_grad * query_f).astype(jnp.bfloat16)
    lower_rim = passed_along(inner[tok_rows - rim_len :], "ctx", 1)
    upper_rim = passed_along(conv_grad[:rim_len], "ctx", -1)
    inner_ext = jnp.concatenate([lower_rim, inner], axis=0).reshape(
        span_width, group_count, group_size
    )
    forward_first = jnp.concatenate(
        [filters[:, ::-1], jnp.zeros((group_count, tok_rows - 1), filters.dtype)], axis=1
    )
    forward_table = toeplitz(forward_first, tok_rows, span_width)
    conv_out = jnp.einsum(
        "gts,sgc->tgc", forward_table, inner_ext, preferred_element_type=jnp.float32
    )
    inner_f = inner.astype(jnp.float32)
    mixed = conv_out.reshape(tok_rows, chan_width) + skip_bias[None, :] * inner_f
    gated = (query_f * mixed).astype(jnp.bfloat16)
    query_grad = (mixed_grad * mixed).astype(jnp.bfloat16)
    grad_ext = jnp.concatenate([conv_grad, upper_rim], axis=0).reshape(
        span_width, group_count, group_size
    )
    backward_first = jnp.concatenate(
        [filters, jnp.zeros((group_count, tok_rows - 1), filters.dtype)], axis=1
    )
    backward_table = toeplitz(backward_first, tok_rows, span_width)
    back_out = jnp.einsum(
        "gsp,pgc->sgc", backward_table, grad_ext, preferred_element_type=jnp.float32
    )
    conv_f = conv_grad.astype(jnp.float32)
    inner_grad = back_out.reshape(tok_rows, chan_width) + skip_bias[None, :] * conv_f
    key_grad = (inner_grad * value_f).astype(jnp.bfloat16)
    value_grad = (inner_grad * key_f).astype(jnp.bfloat16)
    block_count = tok_rows // tap_count
    window_len = tap_count + rim_len
    grad_blocks = conv_grad.reshape(block_count, tap_count, group_count, group_size)
    windows = jnp.stack([inner_ext])
    products = jnp.einsum(
        "btgc,bsgc->bgts", grad_blocks, windows, preferred_element_type=jnp.float32
    )
    flat = products.reshape(block_count, group_count, tap_count * window_len)
    flat = jnp.concatenate(
        [flat, jnp.zeros((block_count, group_count, tap_count), jnp.float32)], axis=2
    )
    skewed = flat.reshape(block_count, group_count, tap_count, window_len + 1)
    diagonals = jnp.sum(skewed[:, :, :, :tap_count], axis=(0, 2))
    local_filter = diagonals[:, ::-1]
    local_skip = jnp.sum(conv_f * inner_f, axis=0)
    filter_grad, skip_grad = lax.psum((local_filter, local_skip), "ctx")
    return (gated, query_grad, key_grad, value_grad, filter_grad, skip_grad)


def solution(mesh):
    in_specs = (
        P("ctx", "ch"),
        P("ctx", "ch"),
        P("ctx", "ch"),
        P("ch", None),
        P("ch"),
        P("ch", None),
        P("ctx", "ch"),
    )
    out_specs = (
        P("ctx", "ch"),
        P("ctx", "ch"),
        P("ctx", "ch"),
        P("ctx", "ch"),
        P("ch", None),
        P("ch"),
    )
    return jax.shard_map(
        per_device, mesh=mesh, in_specs=in_specs, out_specs=out_specs, check_vma=False
    )
```

profile of v0, /device:TPU:0, one launch (start us, length us, event | category | flops | bytes accessed | tf_op | source)
XLA Modules:
  0.0 170.1 jit_solution(13192712764636323653)
XLA Ops:
  7.2 0.7 all-gather.2.cloned.1.call-update
  7.9 27.0 %all-gather.2.cloned.1.call-done = bf16[128,8192]{1,0:T(8,128)(2,1)} async-done(((bf16[128,2048]{1,0:T(8,128)(2,1)}), bf16[128,8192]{1,0:T(8,128)(2,1)}) %all-gather.2.cloned.1.call-update) | async-done | bytes 2097168 | tf_op jit(solution)/shard_map/all_gather | solution.py:31
  34.9 12.2 %fusion.7 = (f32[1024]{0:T(1024)S(1)}, bf16[128,1024]{1,0:T(8,128)(2,1)S(1)}, bf16[128,1024]{1,0:T(8,128)(2,1)S(1)}, f32[128,1024]{1,0:T(8,128)S(1)}) fusion(bf16[128,1024]{1,0:T(8,128)(2,1)} %param.7, bf16[128,1024]{1,0:T(8,128)(2,1)} %param.9, bf16[128,1024]{1,0:T(8,128)(2,1)} %param.8, bf16[128,8192]{1,0:T(8,128)(2,1)} %all-gather.2.cloned.1.call-done, ...), kind=kOutput, calls=%fused_computation.16 | convolution fusion | flops 2148924416 | bytes 20713472 | tf_op jit(solution)/shard_map/dot_general | solution.py:30
  47.1 0.1 slice.20
  47.2 3.4 %collective-permute-start = (bf16[127,1024]{1,0:T(8,128)(2,1)S(1)}, bf16[127,1024]{1,0:T(8,128)(2,1)S(1)}, u32[]{:S(2)}, u32[]{:S(2)}) collective-permute-start(bf16[127,1024]{1,0:T(8,128)(2,1)S(1)} %slice.20), channel_id=1, source_target_pairs={{0,4},{4,8},{8,12},{12,16},{16,20},{20,24},{24,28},{1,5},{5,9},{9,... | collective-permute-start | bytes 780296 | tf_op jit(solution)/shard_map/ppermute | solution.py:10
  50.6 0.1 pad.8.clone
  50.7 0.1 rev.6
  50.8 1.3 collective-permute-start.1
  52.1 0.3 tile.20
  52.4 2.6 %copy.24 = bf16[8,8,128,256]{3,1,2,0:T(8,128)(2,1)S(1)} copy(bf16[8,8,128,256]{3,2,1,0:T(8,128)(2,1)S(1)} %bitcast.29) | data formatting | bytes 8388608
  55.0 2.2 %slice.23 = bf16[64,32640]{1,0:T(8,128)(2,1)} slice(bf16[64,32768]{1,0:T(8,128)(2,1)S(1)} %bitcast.31), slice={[0:64], [0:32640]} | slice | bytes 8355840 | tf_op jit(solution)/shard_map/slice | solution.py:17
  57.2 15.8 %reshape.58 = bf16[64,128,255]{2,1,0:T(8,128)(2,1)} reshape(bf16[64,32640]{1,0:T(8,128)(2,1)} %slice.23) | data formatting | bytes 8355840 | tf_op jit(solution)/shard_map/reshape | solution.py:17
  73.1 0.3 tile.8
  73.3 2.6 %copy.23 = bf16[8,8,128,256]{3,1,2,0:T(8,128)(2,1)S(1)} copy(bf16[8,8,128,256]{3,2,1,0:T(8,128)(2,1)S(1)} %bitcast.30) | data formatting | bytes 8388608
  76.0 2.2 %slice.21 = bf16[64,32640]{1,0:T(8,128)(2,1)} slice(bf16[64,32768]{1,0:T(8,128)(2,1)S(1)} %bitcast.32), slice={[0:64], [0:32640]} | slice | bytes 8355840 | tf_op jit(solution)/shard_map/slice | solution.py:17
  78.2 15.9 %reshape.55 = bf16[64,128,255]{2,1,0:T(8,128)(2,1)} reshape(bf16[64,32640]{1,0:T(8,128)(2,1)} %slice.21) | data formatting | bytes 8355840 | tf_op jit(solution)/shard_map/reshape | solution.py:17
  94.0 0.2 copy.22
  94.2 0.1 pad_maximum_fusion
  94.3 0.2 copy.18
  94.5 0.2 copy.20
  94.8 3.4 %fusion.11 = f32[64,16,128]{2,1,0:T(8,128)S(1)} fusion(bf16[255,64,16]{0,2,1:T(8,128)(2,1)S(1)} %bitcast.36, bf16[64,128,255]{2,1,0:T(8,128)(2,1)} %reshape.58), kind=kOutput, calls=%fused_computation.23 | convolution fusion | flops 66846720 | bytes 5224448 | tf_op jit(solution)/shard_map/gsp,pgc->sgc/dot_general | solution.py:60
  98.1 0.2 copy.21
  98.3 3.4 %fusion.10 = f32[64,16,128]{2,1,0:T(8,128)S(1)} fusion(bf16[255,64,16]{0,2,1:T(8,128)(2,1)S(1)} %bitcast.33, bf16[64,128,255]{2,1,0:T(8,128)(2,1)} %reshape.55), kind=kOutput, calls=%fused_computation.22 | convolution fusion | flops 66846720 | bytes 5224448 | tf_op jit(solution)/shard_map/gts,sgc->tgc/dot_general | solution.py:46
  101.7 0.2 copy.19
  101.9 4.5 %fusion.12 = f32[64,128,255]{2,1,0:T(8,128)} fusion(bf16[128,64,16]{0,2,1:T(8,128)(2,1)S(1)} %bitcast.39, bf16[255,64,16]{0,2,1:T(8,128)(2,1)S(1)} %bitcast.34), kind=kOutput, calls=%fused_computation.24 | convolution fusion | flops 66846720 | bytes 9140224 | tf_op jit(solution)/shard_map/btgc,bsgc->bgts/dot_general | solution.py:71
  106.5 9.2 %reshape.61 = f32[1,64,32640]{2,1,0:T(8,128)} reshape(f32[64,128,255]{2,1,0:T(8,128)} %fusion.12) | data formatting | bytes 16711680 | tf_op jit(solution)/shard_map/reshape | solution.py:74
  115.7 4.0 %concatenate.19 = f32[1,64,32768]{2,1,0:T(8,128)S(1)} pad(f32[1,64,32640]{2,1,0:T(8,128)} %reshape.61, f32[]{:T(128)} %constant.3.clone.1), padding=0_0x0_0x0_128 | pad | bytes 16744452 | tf_op jit(solution)/shard_map/concatenate | solution.py:75
  119.7 2.5 %copy.25 = f32[8,8,128,256]{3,2,1,0:T(8,128)S(1)} copy(f32[8,8,128,256]{3,1,2,0:T(8,128)S(1)} %bitcast.27) | data formatting | bytes 16777216
  122.3 0.5 slice_reduce_fusion
  122.8 0.1 rev.7
  122.9 39.2 %all-reduce.1 = (f32[64,128]{1,0:T(8,128)}, f32[1024]{0:T(1024)}) all-reduce(f32[64,128]{1,0:T(8,128)S(1)} %rev.7, f32[1024]{0:T(1024)S(1)} %get-tuple-element.8), channel_id=1, replica_groups=mesh['ctx'=8,'ch'=4] {'ctx'}, use_global_device_ids=true, to_apply=%region_1.0 | all-reduce | flops 9216 | bytes 73728 | tf_op jit(solution)/shard_map/psum | solution.py:82
  162.1 1.2 fusion.2
  (17 shorter events, 0.1 us)
Async XLA Ops:
  7.2 27.7 %all-gather.2.cloned.1.call-start = ((), (), s32[]{:S(2)}) async-start(), calls=%async_computation | async-start | bytes 2621440 | tf_op jit(solution)/shard_map/all_gather | solution.py:31
  7.9 42.8 %copy-start.3 = (bf16[64,128]{1,0:T(8,128)(2,1)S(1)}, bf16[64,128]{1,0:T(8,128)(2,1)}, u32[]{:S(2)}) copy-start(bf16[64,128]{1,0:T(8,128)(2,1)} %param.10) | copy-start | bytes 49156
  47.2 47.0 %collective-permute-start = (bf16[127,1024]{1,0:T(8,128)(2,1)S(1)}, bf16[127,1024]{1,0:T(8,128)(2,1)S(1)}, u32[]{:S(2)}, u32[]{:S(2)}) collective-permute-start(bf16[127,1024]{1,0:T(8,128)(2,1)S(1)} %slice.20), channel_id=1, source_target_pairs={{0,4},{4,8},{8,12},{12,16},{16,20},{20,24},{24,28},{1,5},{5,9},{9,... | collective-permute-start | bytes 780296 | tf_op jit(solution)/shard_map/ppermute | solution.py:10
  50.8 43.7 %collective-permute-start.1 = (bf16[127,1024]{1,0:T(8,128)(2,1)S(1)}, bf16[127,1024]{1,0:T(8,128)(2,1)S(1)}, u32[]{:S(2)}, u32[]{:S(2)}) collective-permute-start(bf16[127,1024]{1,0:T(8,128)(2,1)S(1)} %bitcast.35), channel_id=1, source_target_pairs={{4,0},{8,4},{12,8},{16,12},{20,16},{24,20},{28,24},{5,1},{9,5},{13... | collective-permute-start | bytes 780296 | tf_op jit(solution)/shard_map/ppermute | solution.py:10
  122.3 39.8 %copy-start = (bf16[128,1024]{1,0:T(8,128)(2,1)S(1)}, bf16[128,1024]{1,0:T(8,128)(2,1)}, u32[]{:S(2)}) copy-start(bf16[128,1024]{1,0:T(8,128)(2,1)} %param.8) | copy-start | bytes 786436
  122.3 39.8 %copy-start.1 = (bf16[128,1024]{1,0:T(8,128)(2,1)S(1)}, bf16[128,1024]{1,0:T(8,128)(2,1)}, u32[]{:S(2)}) copy-start(bf16[128,1024]{1,0:T(8,128)(2,1)} %param.7) | copy-start | bytes 786436
  122.3 39.8 %copy-start.2 = (bf16[128,1024]{1,0:T(8,128)(2,1)S(1)}, bf16[128,1024]{1,0:T(8,128)(2,1)}, u32[]{:S(2)}) copy-start(bf16[128,1024]{1,0:T(8,128)(2,1)} %param.9) | copy-start | bytes 786436
  122.3 39.8 %copy-start.4 = (f32[1024]{0:T(1024)S(1)}, f32[1024]{0:T(1024)}, u32[]{:S(2)}) copy-start(f32[1024]{0:T(1024)} %param.11) | copy-start | bytes 12292
Sparse Core Ops, SparseCore 0:
  9.6 25.2 all-gather.1
where the time goes:
time: 171 us; the launch traced here: 170 us
  local copies, waits for them, and re-layouts  59 us (35%)
  blocking collectives  39.2 us (23%)
  waiting for transfers between devices  27.7 us (16%)
  matrix products  23.5 us (14%)
  between operations  14.2 us (8%)
  starting transfers between devices  4.71 us (3%)
  other arithmetic  1.88 us (1%)
    psum x1, blocking collectives, per_device(): filter_grad, skip_grad = lax.psum((local_filter, local_skip), 'ctx')  39.2 us
    reshape x2, local copies, waits for them, and re-layouts, toeplitz(): tiled[:, :tok_rows * span_width].reshape(group_count, tok_rows, span_width)  31.7 us
    all_gather x1, waiting for transfers between devices, per_device(): lax.all_gather(out_grad, 'ch', axis=1, tiled=True)  27 us
    dot_general x1, matrix products, per_device(): lax.dot_general(lax.all_gather(out_grad, 'ch', axis=1, tiled=True), out_w...  12.2 us
    reshape x1, local copies, waits for them, and re-layouts, per_device(): flat = products.reshape(block_count, group_count, tap_count * window_len)  9.23 us
    unnamed x13, local copies, waits for them, and re-layouts  7.75 us
    ppermute x2, starting transfers between devices, passed_along(): return lax.ppermute(block, axis, route)  4.67 us
    dot_general x1, matrix products, per_device(): jnp.einsum('btgc,bsgc->bgts', grad_blocks, windows, preferred_element_typ...  4.53 us
  transfers between devices with their start and end apart: 3, of which 1 were waited for; matrix products, arithmetic and copies ran while one was open for 25% of the time, Pallas kernels for 0%

commit v1 on v0

v1 whole, which is shorter than its diff:
```python
import functools

import jax
import jax.numpy as jnp
from jax import lax
from jax.experimental import pallas as pl
from jax.experimental.pallas import tpu as pltpu
from jax.sharding import PartitionSpec as P

LANES = 128
PIECE = 256
MESH = pl.DeviceIdType.MESH
F32 = jnp.float32
BF16 = jnp.bfloat16
NT = (((1,), (1,)), ((), ()))


def kernel_body(n_ctx, n_ch, reduce_here, *refs):
    (q_ref, k_ref, v_ref, f_ref, skip_ref, w_ref, og_ref,
     gated_ref, qg_ref, kg_ref, vg_ref, fg_ref, sg_ref,
     og_all, w_all, table_f, table_b, fl_ref, inner_ext, inner_rev,
     acc_ref, mixed_ref, grad_ext, ig_ref, part_ref, got_ref, red_ref, all_ref,
     w_sem, own_sem, y_send, y_recv, core_send, core_recv, fwd_send, fwd_recv,
     rim_send, rim_recv, up_send, up_recv, p1_send, p1_recv, p2_send, p2_recv) = refs
    tok, chan = q_ref.shape
    groups, taps = f_ref.shape
    gsize = chan // groups
    per_tile = LANES // gsize
    tiles = chan // LANES
    kb = og_ref.shape[1]
    n_pieces = kb // PIECE
    n_chips = n_ch // 2

    ctx = lax.axis_index("ctx")
    ch = lax.axis_index("ch")
    chip, core = ch // 2, ch % 2
    sibling = chip * 2 + (1 - core)
    first, last = ctx == 0, ctx == n_ctx - 1

    barrier = pltpu.get_barrier_semaphore()
    if reduce_here:
        offsets = list(range(1, n_ctx))
    else:
        offsets = sorted({1, n_ctx - 1})
    for d in offsets:
        pl.semaphore_signal(barrier, inc=1, device_id={"ctx": lax.rem(ctx + d, n_ctx)}, device_id_type=MESH)
    pl.semaphore_signal(barrier, inc=1, device_id={"ch": sibling}, device_id_type=MESH)
    for d in range(1, n_chips):
        other = lax.rem(chip + d, n_chips) * 2 + core
        pl.semaphore_signal(barrier, inc=1, device_id={"ch": other}, device_id_type=MESH)

    def owner_of(index):
        if index == 0:
            return ch
        if index == 1:
            return sibling
        d, other = (index - 2) // 2 + 1, (index - 2) % 2
        base = lax.rem(chip - d + n_chips, n_chips) * 2
        return base + (core if other == 0 else 1 - core)

    def w_copy(index):
        cols = pl.ds(pl.multiple_of(owner_of(index) * kb, LANES), kb)
        return pltpu.make_async_copy(w_ref.at[:, cols], w_all.at[index], w_sem.at[index])

    own_copy = pltpu.make_async_copy(og_ref, og_all.at[ch], own_sem)
    own_copy.start()
    for index in range(n_ch):
        w_copy(index).start()

    pl.semaphore_wait(barrier, len(offsets) + 1 + n_chips - 1)

    def y_copy(d, p):
        cols = pl.ds(p * PIECE, PIECE)
        other = lax.rem(chip + d, n_chips) * 2 + core
        return pltpu.make_async_remote_copy(
            og_ref.at[:, cols], og_all.at[ch, :, cols], y_send.at[d - 1, p], y_recv.at[d - 1, p],
            device_id={"ch": other}, device_id_type=MESH)

    def fwd_copy(d, p):
        cols = pl.ds(p * PIECE, PIECE)
        owner = lax.rem(chip - d + n_chips, n_chips) * 2 + core
        piece = og_all.at[owner, :, cols]
        return pltpu.make_async_remote_copy(
            piece, piece, fwd_send.at[d - 1, p], fwd_recv.at[d - 1, p],
            device_id={"ch": sibling}, device_id_type=MESH)

    core_copy = pltpu.make_async_remote_copy(
        og_ref, og_all.at[ch], core_send, core_recv, device_id={"ch": sibling}, device_id_type=MESH)
    for p in range(n_pieces):
        for d in range(1, n_chips):
            y_copy(d, p).start()
    core_copy.start()

    inner_ext[tok:, :] = (k_ref[...].astype(F32) * v_ref[...].astype(F32)).astype(BF16)

    def rim_copy():
        return pltpu.make_async_remote_copy(
            inner_ext.at[pl.ds(tok, tok)], inner_ext.at[pl.ds(0, tok)], rim_send, rim_recv,
            device_id={"ctx": lax.rem(ctx + 1, n_ctx)}, device_id_type=MESH)

    @pl.when(jnp.logical_not(last))
    def _():
        rim_copy().start()

    @pl.when(first)
    def _():
        inner_ext[:tok, :] = jnp.zeros((tok, chan), BF16)

    @pl.when(last)
    def _():
        grad_ext[tok:, :] = jnp.zeros((tok, chan), BF16)

    row = lax.broadcasted_iota(jnp.int32, (tok, taps), 0)
    col = lax.broadcasted_iota(jnp.int32, (tok, taps), 1)
    negate = (lax.rem(row + col, taps) == 0).astype(BF16)
    flip = (row + col == taps - 1).astype(BF16)
    filt = f_ref[...]
    fl_ref[0] = filt.astype(F32)
    fl_ref[1] = jnp.dot(filt, negate, preferred_element_type=F32)

    def build(g, carry):
        rows = pl.ds(pl.multiple_of(g * tok, tok), tok)
        back = jnp.broadcast_to(fl_ref[0, pl.ds(g, 1), :], (tok, taps))
        back = pltpu.roll(back, 0, 1, stride=1, stride_axis=0)
        table_b[rows, :taps] = jnp.where(col >= row, back, 0.0).astype(BF16)
        table_b[rows, taps:] = jnp.where(col < row, back, 0.0).astype(BF16)
        fwd = jnp.broadcast_to(fl_ref[1, pl.ds(g, 1), :], (tok, taps))
        fwd = pltpu.roll(fwd, 0, 1, stride=1, stride_axis=0)
        table_f[rows, :taps] = jnp.where(col > row, fwd, 0.0).astype(BF16)
        table_f[rows, taps:] = jnp.where(col <= row, fwd, 0.0).astype(BF16)
        return carry

    lax.fori_loop(0, groups, build, 0)

    def multiply(index, owner, p, fresh=False):
        cols = pl.ds(pl.multiple_of(p * PIECE, PIECE), PIECE)
        product = lax.dot_general(
            w_all[index, :, cols], og_all[owner, :, cols], NT, preferred_element_type=F32)
        acc_ref[...] += product

    def multiply_block(index, owner):
        lax.fori_loop(0, n_pieces, lambda p, c: (multiply(index, owner, p), c)[1], 0)

    acc_ref[...] = jnp.zeros_like(acc_ref)
    own_copy.wait()
    w_copy(0).wait()
    multiply_block(0, ch)
    core_copy.wait_recv()
    w_copy(1).wait()
    multiply_block(1, sibling)

    lane_group = lax.broadcasted_iota(jnp.int32, (tok, LANES), 1) // gsize

    def pick(result):
        out = result[:tok]
        for i in range(1, per_tile):
            out = jnp.where(lane_group == i, result[i * tok:(i + 1) * tok], out)
        return out

    def tile_rows(k):
        return pl.ds(pl.multiple_of(k * per_tile * tok, per_tile * tok), per_tile * tok)

    def tile_lanes(k):
        return pl.ds(pl.multiple_of(k * LANES, LANES), LANES)

    @pl.when(jnp.logical_not(first))
    def _():
        rim_copy().wait_recv()

    def forward(k, carry):
        lanes = tile_lanes(k)
        result = jnp.dot(table_f[tile_rows(k), :], inner_ext[:, lanes], preferred_element_type=F32)
        mixed = pick(result) + skip_ref[:, lanes] * inner_ext[tok:, lanes].astype(F32)
        mixed_ref[:, lanes] = mixed
        gated_ref[:, lanes] = (q_ref[:, lanes].astype(F32) * mixed).astype(BF16)
        inner_rev[:tok, lanes] = jnp.dot(flip, inner_ext[:tok, lanes], preferred_element_type=F32).astype(BF16)
        inner_rev[tok:, lanes] = jnp.dot(flip, inner_ext[tok:, lanes], preferred_element_type=F32).astype(BF16)
        return carry

    lax.fori_loop(0, tiles, forward, 0)

    for index in range(2, n_ch):
        w_copy(index).wait()
    for p in range(n_pieces):
        for d in range(1, n_chips):
            y_copy(d, p).wait_recv()
            fwd_copy(d, p).start()
            multiply(2 * d, owner_of(2 * d), p)
            if p > 0:
                fwd_copy(d, p - 1).wait_recv()
                multiply(2 * d + 1, owner_of(2 * d + 1), p - 1)
    for d in range(1, n_chips):
        fwd_copy(d, n_pieces - 1).wait_recv()
        multiply(2 * d + 1, owner_of(2 * d + 1), n_pieces - 1)

    def up_copy(k):
        lanes = pl.ds(k * LANES, LANES)
        return pltpu.make_async_remote_copy(
            grad_ext.at[pl.ds(0, tok), lanes], grad_ext.at[pl.ds(tok, tok), lanes],
            up_send.at[k], up_recv.at[k],
            device_id={"ctx": lax.rem(ctx + n_ctx - 1, n_ctx)}, device_id_type=MESH)

    for k in range(tiles):
        lanes = pl.ds(k * LANES, LANES)
        mg = acc_ref[k * LANES:(k + 1) * LANES, :].T
        grad_ext[:tok, lanes] = (mg * q_ref[:, lanes].astype(F32)).astype(BF16)

        @pl.when(jnp.logical_not(first))
        def _():
            up_copy(k).start()

        qg_ref[:, lanes] = (mg * mixed_ref[:, lanes]).astype(BF16)

    def gradients(k, carry):
        lanes = tile_lanes(k)
        cg = grad_ext[:tok, lanes]
        zero = jnp.zeros_like(cg)
        masked = jnp.concatenate([jnp.where(lane_group == i, cg, zero) for i in range(per_tile)], axis=0)
        pairs = lax.dot_general(masked, inner_rev[:, lanes], NT, preferred_element_type=F32)
        sums = []
        for i in range(per_tile):
            block = pairs[i * tok:(i + 1) * tok]
            block = jnp.where(row + col >= taps - 1, block[:, taps:], block[:, :taps])
            block = pltpu.roll(block, 1, 1, stride=1, stride_axis=0)
            sums.append(jnp.sum(block, axis=0, keepdims=True))
        part_ref[k, :per_tile, :] = jnp.concatenate(sums, axis=0)
        skip = jnp.sum(cg.astype(F32) * inner_ext[tok:, lanes].astype(F32), axis=0, keepdims=True)
        part_ref[k, per_tile:, :] = jnp.broadcast_to(skip, (per_tile, LANES))
        return carry

    lax.fori_loop(0, tiles, gradients, 0)

    def p1_copy(d):
        target = lax.rem(ctx + d, n_ctx)
        return pltpu.make_async_remote_copy(
            part_ref.at[target], got_ref.at[d], p1_send.at[d], p1_recv.at[d],
            device_id={"ctx": target}, device_id_type=MESH)

    def p2_copy(d):
        target = lax.rem(ctx + d, n_ctx)
        return pltpu.make_async_remote_copy(
            red_ref, all_ref.at[ctx], p2_send.at[d], p2_recv.at[d],
            device_id={"ctx": target}, device_id_type=MESH)

    if reduce_here:
        for d in range(1, n_ctx):
            p1_copy(d).start()

    def backward(k, carry):
        lanes = tile_lanes(k)
        cg = grad_ext[:tok, lanes]
        result = jnp.dot(table_b[tile_rows(k), :taps], cg, preferred_element_type=F32)
        ig_ref[:, lanes] = pick(result) + skip_ref[:, lanes] * cg.astype(F32)
        return carry

    lax.fori_loop(0, tiles, backward, 0)

    if reduce_here:
        total = part_ref[ctx]
        for d in range(1, n_ctx):
            p1_copy(d).wait_recv()
            total = total + got_ref[d]
        red_ref[...] = total
        for d in range(1, n_ctx):
            p2_copy(d).start()

    for k in range(tiles):
        lanes = pl.ds(k * LANES, LANES)

        @pl.when(jnp.logical_not(last))
        def _():
            up_copy(k).wait_recv()

        rows = pl.ds(k * per_tile * tok, per_tile * tok)
        result = jnp.dot(table_b[rows, taps:], grad_ext[tok:, lanes], preferred_element_type=F32)
        ig = ig_ref[:, lanes] + pick(result)
        kg_ref[:, lanes] = (ig * v_ref[:, lanes].astype(F32)).astype(BF16)
        vg_ref[:, lanes] = (ig * k_ref[:, lanes].astype(F32)).astype(BF16)

    def write_sums(k, values):
        fg_ref[k] = values[:per_tile]
        sg_ref[k] = values[per_tile:per_tile + 1]

    if reduce_here:
        all_ref[ctx] = red_ref[...]
        for d in range(1, n_ctx):
            p2_copy(d).wait_recv()
        for k in range(tiles):
            write_sums(k, all_ref[k])
        for d in range(1, n_ctx):
            p1_copy(d).wait_send()
            p2_copy(d).wait_send()
    else:
        for k in range(tiles):
            write_sums(k, part_ref[k])

    core_copy.wait_send()
    for p in range(n_pieces):
        for d in range(1, n_chips):
            y_copy(d, p).wait_send()
            fwd_copy(d, p).wait_send()

    @pl.when(jnp.logical_not(last))
    def _():
        rim_copy().wait_send()

    @pl.when(jnp.logical_not(first))
    def _():
        for k in range(tiles):
            up_copy(k).wait_send()


def per_device(n_ctx, n_ch, query_act, key_act, value_act, filters, skip_bias, out_weight, out_grad):
    tok, chan = query_act.shape
    groups, taps = filters.shape
    kb = out_grad.shape[1]
    tiles = chan // LANES
    per_tile = LANES * groups // chan
    n_pieces = kb // PIECE
    n_hops = max(n_ch // 2 - 1, 1)
    reduce_here = tiles == n_ctx
    dma = pltpu.SemaphoreType.DMA
    vmem = pl.BlockSpec(memory_space=pltpu.VMEM)
    hbm = pl.BlockSpec(memory_space=pl.ANY)
    n_slots = n_ctx if reduce_here else 1
    act = jax.ShapeDtypeStruct((tok, chan), BF16)
    outs = pl.pallas_call(
        functools.partial(kernel_body, n_ctx, n_ch, reduce_here),
        out_shape=(
            act, act, act, act,
            jax.ShapeDtypeStruct((tiles, per_tile, LANES), F32),
            jax.ShapeDtypeStruct((tiles, 1, LANES), F32),
        ),
        in_specs=[vmem] * 5 + [hbm] * 2,
        out_specs=(vmem,) * 6,
        scratch_shapes=[
            pltpu.VMEM((n_ch, tok, kb), BF16),
            pltpu.VMEM((n_ch, chan, kb), BF16),
            pltpu.VMEM((groups * tok, 2 * taps), BF16),
            pltpu.VMEM((groups * tok, 2 * taps), BF16),
            pltpu.VMEM((2, groups, taps), F32),
            pltpu.VMEM((2 * tok, chan), BF16),
            pltpu.VMEM((2 * tok, chan), BF16),
            pltpu.VMEM((chan, tok), F32),
            pltpu.VMEM((tok, chan), F32),
            pltpu.VMEM((2 * tok, chan), BF16),
            pltpu.VMEM((tok, chan), F32),
            pltpu.VMEM((tiles, 2 * per_tile, LANES), F32),
            pltpu.VMEM((n_slots, 2 * per_tile, LANES), F32),
            pltpu.VMEM((2 * per_tile, LANES), F32),
            pltpu.VMEM((n_slots, 2 * per_tile, LANES), F32),
            dma((n_ch,)), dma,
            dma((n_hops, n_pieces)), dma((n_hops, n_pieces)),
            dma, dma,
            dma((n_hops, n_pieces)), dma((n_hops, n_pieces)),
            dma, dma,
            dma((tiles,)), dma((tiles,)),
            dma((n_slots,)), dma((n_slots,)), dma((n_slots,)), dma((n_slots,)),
        ],
        compiler_params=pltpu.CompilerParams(
            collective_id=0, has_side_effects=True, vmem_limit_bytes=56 * 2**20),
        name="hyena",
    )(query_act, key_act, value_act, filters, skip_bias.reshape(1, chan), out_weight, out_grad)
    gated, query_grad, key_grad, value_grad, filter_grad, skip_grad = outs
    filter_grad = filter_grad.reshape(groups, taps)
    skip_grad = skip_grad.reshape(chan)
    if not reduce_here:
        filter_grad, skip_grad = lax.psum((filter_grad, skip_grad), "ctx")
    return gated, query_grad, key_grad, value_grad, filter_grad, skip_grad


def solution(mesh):
    act = P("ctx", "ch")
    in_specs = (act, act, act, P("ch", None), P("ch"), P("ch", None), act)
    out_specs = (act, act, act, act, P("ch", None), P("ch"))
    return jax.shard_map(
        functools.partial(per_device, mesh.shape["ctx"], mesh.shape["ch"]),
        mesh=mesh, in_specs=in_specs, out_specs=out_specs, check_vma=False,
    )
```

time: 171 us -> 52.2 us (0.31)
  local copies, waits for them, and re-layouts: 59 us -> 9.32 us
  Pallas kernels: 0 us -> 41.9 us
  blocking collectives: 39.2 us -> 0 us
  waiting for transfers between devices: 27.7 us -> 0 us
  matrix products: 23.5 us -> 0 us
  between operations: 14.2 us -> 0.64 us
  starting transfers between devices: 4.71 us -> 0 us
  other arithmetic: 1.88 us -> 0 us
    pallas_call x0 -> x1, Pallas kernels: none -> 41.9 us  [per_device(): pl.pallas_call(functools.partial(kernel_body, n_ctx, n_ch, reduce_here),...]
    reshape x5 -> x0, local copies, waits for them, and re-layouts: 41.4 us -> none  [the longest x2 31.7 us: toeplitz(): tiled[:, :tok_rows * span_width].reshape(group_count, tok_rows, span_width)]
    psum x1 -> x0, blocking collectives: 39.2 us -> none  [per_device(): filter_grad, skip_grad = lax.psum((local_filter, local_skip), 'ctx')]
    all_gather x1 -> x0, waiting for transfers between devices: 27 us -> none  [per_device(): lax.all_gather(out_grad, 'ch', axis=1, tiled=True)]
    dot_general x4 -> x0, matrix products: 23.5 us -> none  [the longest x1 12.2 us: per_device(): lax.dot_general(lax.all_gather(out_grad, 'ch', axis=1, tiled=True), out_w...]
    ppermute x2 -> x0, starting transfers between devices: 4.67 us -> none  [passed_along(): return lax.ppermute(block, axis, route)]
    concatenate x5 -> x0, local copies, waits for them, and re-layouts: 4.53 us -> none  [the longest x1 4.04 us: per_device(): jnp.concatenate([flat, jnp.zeros((block_count, group_count, tap_count), j...]
    slice x3 -> x0, local copies, waits for them, and re-layouts: 4.5 us -> none  [the longest x2 4.44 us: toeplitz(): tiled[:, :tok_rows * span_width].reshape(group_count, tok_rows, span_width)]
  transfers between devices with their start and end apart: 3 -> 0, of which waited for: 1 -> 0; matrix products, arithmetic and copies ran while one was open for 25% -> 0% of each run, Pallas kernels for 0% -> 0%
where the time goes in v1:
time: 52.2 us; the launch traced here: 51.8 us
  Pallas kernels  41.9 us (80%)
  local copies, waits for them, and re-layouts  9.32 us (18%)
  between operations  0.64 us (1%)
    pallas_call x1, Pallas kernels, per_device(): pl.pallas_call(functools.partial(kernel_body, n_ctx, n_ch, reduce_here),...  41.9 us
    unnamed x6, local copies, waits for them, and re-layouts  9.32 us

profile of v1, /device:TPU:0, one launch (start us, length us, event | category | flops | bytes accessed | tf_op | source)
XLA Modules:
  0.0 51.8 jit_solution(6323364994249799141)
XLA Ops:
  0.6 41.9 %hyena.1 = (bf16[128,1024]{1,0:T(8,128)(2,1)}, bf16[128,1024]{1,0:T(8,128)(2,1)}, bf16[128,1024]{1,0:T(8,128)(2,1)}, bf16[128,1024]{1,0:T(8,128)(2,1)}, f32[8,8,128]{2,1,0:T(8,128)}, /*index=5*/f32[8,1,128]{2,1,0:T(1,128)}) custom-call(bf16[128,1024]{1,0:T(8,128)(2,1)} %refs_0_.1, bf16[128,1024]{1,0:T(8,128)(2,1)} %refs_1_.1, bf16[128,1024]{1,0:T(8,128)(2,1)} %refs_2_.1, ...), custom_call_target="tpu_custom_call" | custom-call | tf_op jit(solution)/shard_map/hyena/pallas_call | solution.py:327
  42.5 1.7 %copy.19 = bf16[128,1024]{1,0:T(8,128)(2,1)} copy(bf16[128,1024]{1,0:T(8,128)(2,1)} %get-tuple-element.24) | data formatting | bytes 524288
  44.2 1.7 %copy.20 = bf16[128,1024]{1,0:T(8,128)(2,1)} copy(bf16[128,1024]{1,0:T(8,128)(2,1)} %get-tuple-element.25) | data formatting | bytes 524288
  45.9 1.7 %copy.21 = bf16[128,1024]{1,0:T(8,128)(2,1)} copy(bf16[128,1024]{1,0:T(8,128)(2,1)} %get-tuple-element.26) | data formatting | bytes 524288
  47.5 1.7 %copy.22 = bf16[128,1024]{1,0:T(8,128)(2,1)} copy(bf16[128,1024]{1,0:T(8,128)(2,1)} %get-tuple-element.27) | data formatting | bytes 524288
  49.2 1.4 %copy.23 = f32[64,128]{1,0:T(8,128)} copy(f32[64,128]{1,0:T(8,128)} %bitcast.3) | data formatting | bytes 65536
  50.6 1.3 %copy.24 = f32[1024]{0:T(1024)} copy(f32[1024]{0:T(1024)} %bitcast.4) | data formatting | bytes 8192

commit v2 on v1

--- a/solution.py
+++ b/solution.py
@@ -8,7 +8,7 @@
 from jax.sharding import PartitionSpec as P
 
 LANES = 128
-PIECE = 256
+PIECE = 1024
 MESH = pl.DeviceIdType.MESH
 F32 = jnp.float32
 BF16 = jnp.bfloat16
@@ -120,10 +120,6 @@
 
     def build(g, carry):
         rows = pl.ds(pl.multiple_of(g * tok, tok), tok)
-        back = jnp.broadcast_to(fl_ref[0, pl.ds(g, 1), :], (tok, taps))
-        back = pltpu.roll(back, 0, 1, stride=1, stride_axis=0)
-        table_b[rows, :taps] = jnp.where(col >= row, back, 0.0).astype(BF16)
-        table_b[rows, taps:] = jnp.where(col < row, back, 0.0).astype(BF16)
         fwd = jnp.broadcast_to(fl_ref[1, pl.ds(g, 1), :], (tok, taps))
         fwd = pltpu.roll(fwd, 0, 1, stride=1, stride_axis=0)
         table_f[rows, :taps] = jnp.where(col > row, fwd, 0.0).astype(BF16)
@@ -131,6 +127,14 @@
         return carry
 
     lax.fori_loop(0, groups, build, 0)
+
+    def build_back(g, carry):
+        rows = pl.ds(pl.multiple_of(g * tok, tok), tok)
+        back = jnp.broadcast_to(fl_ref[0, pl.ds(g, 1), :], (tok, taps))
+        back = pltpu.roll(back, 0, 1, stride=1, stride_axis=0)
+        table_b[rows, :taps] = jnp.where(col >= row, back, 0.0).astype(BF16)
+        table_b[rows, taps:] = jnp.where(col < row, back, 0.0).astype(BF16)
+        return carry
 
     def multiply(index, owner, p, fresh=False):
         cols = pl.ds(pl.multiple_of(p * PIECE, PIECE), PIECE)
@@ -246,6 +250,8 @@
         for d in range(1, n_ctx):
             p1_copy(d).start()
 
+    lax.fori_loop(0, groups, build_back, 0)
+
     def backward(k, carry):
         lanes = tile_lanes(k)
         cg = grad_ext[:tok, lanes]
@@ -308,6 +314,17 @@
     def _():
         for k in range(tiles):
             up_copy(k).wait_send()
+
+
+def hand_on(*refs):
+    count = (len(refs) - 1) // 2
+    copies = [
+        pltpu.make_async_copy(refs[i], refs[count + i], refs[-1].at[i]) for i in range(count)
+    ]
+    for copy in copies:
+        copy.start()
+    for copy in copies:
+        copy.wait()
 
 
 def per_device(n_ctx, n_ch, query_act, key_act, value_act, filters, skip_bias, out_weight, out_grad):
@@ -361,6 +378,14 @@
             collective_id=0, has_side_effects=True, vmem_limit_bytes=56 * 2**20),
         name="hyena",
     )(query_act, key_act, value_act, filters, skip_bias.reshape(1, chan), out_weight, out_grad)
+    outs = pl.pallas_call(
+        hand_on,
+        out_shape=tuple(jax.ShapeDtypeStruct(x.shape, x.dtype) for x in outs),
+        in_specs=[vmem] * len(outs),
+        out_specs=(hbm,) * len(outs),
+        scratch_shapes=[dma((len(outs),))],
+        name="hand_on",
+    )(*outs)
     gated, query_grad, key_grad, value_grad, filter_grad, skip_grad = outs
     filter_grad = filter_grad.reshape(groups, taps)
     skip_grad = skip_grad.reshape(chan)

time: 52.2 us -> 42.6 us (0.82)
  local copies, waits for them, and re-layouts: 9.32 us -> 0 us
    unnamed x6 -> x0, local copies, waits for them, and re-layouts: 9.32 us -> none
    pallas_call x1, Pallas kernels: 41.9 us -> 39.6 us  [per_device(): pl.pallas_call(functools.partial(kernel_body, n_ctx, n_ch, reduce_here),...]
    pallas_call x0 -> x1, Pallas kernels: none -> 2.21 us  [per_device(): pl.pallas_call(hand_on, out_shape=tuple((jax.ShapeDtypeStruct(x.shape, x....]
where the time goes in v2:
time: 42.6 us; the launch traced here: 42.4 us
  Pallas kernels  41.8 us (98%)
  between operations  0.64 us (2%)
    pallas_call x1, Pallas kernels, per_device(): pl.pallas_call(functools.partial(kernel_body, n_ctx, n_ch, reduce_here),...  39.6 us
    pallas_call x1, Pallas kernels, per_device(): pl.pallas_call(hand_on, out_shape=tuple((jax.ShapeDtypeStruct(x.shape, x....  2.21 us

profile of v2, /device:TPU:0, one launch (start us, length us, event | category | flops | bytes accessed | tf_op | source)
XLA Modules:
  0.0 42.4 jit_solution(15085441603765936620)
XLA Ops:
  0.6 39.6 %hyena.1 = (bf16[128,1024]{1,0:T(8,128)(2,1)}, bf16[128,1024]{1,0:T(8,128)(2,1)}, bf16[128,1024]{1,0:T(8,128)(2,1)}, bf16[128,1024]{1,0:T(8,128)(2,1)}, f32[8,8,128]{2,1,0:T(8,128)}, /*index=5*/f32[8,1,128]{2,1,0:T(1,128)}) custom-call(bf16[128,1024]{1,0:T(8,128)(2,1)} %refs_0_.1, bf16[128,1024]{1,0:T(8,128)(2,1)} %refs_1_.1, bf16[128,1024]{1,0:T(8,128)(2,1)} %refs_2_.1, ...), custom_call_target="tpu_custom_call" | custom-call | tf_op jit(solution)/shard_map/hyena/pallas_call | solution.py:344
  40.2 2.2 %hand_on.1 = (bf16[128,1024]{1,0:T(8,128)(2,1)}, bf16[128,1024]{1,0:T(8,128)(2,1)}, bf16[128,1024]{1,0:T(8,128)(2,1)}, bf16[128,1024]{1,0:T(8,128)(2,1)}, f32[8,8,128]{2,1,0:T(8,128)}, /*index=5*/f32[8,1,128]{2,1,0:T(1,128)}) custom-call(bf16[128,1024]{1,0:T(8,128)(2,1)} %get-tuple-element.18.refs_0_, bf16[128,1024]{1,0:T(8,128)(2,1)} %get-tuple-element.19.refs_1_, ...), custom_call_target="tpu_custom_call" | custom-call | tf_op jit(solution)/shard_map/hand_on/pallas_call | solution.py:381

commit v3 on v2

--- a/solution.py
+++ b/solution.py
@@ -67,41 +67,7 @@
     for index in range(n_ch):
         w_copy(index).start()
 
-    pl.semaphore_wait(barrier, len(offsets) + 1 + n_chips - 1)
-
-    def y_copy(d, p):
-        cols = pl.ds(p * PIECE, PIECE)
-        other = lax.rem(chip + d, n_chips) * 2 + core
-        return pltpu.make_async_remote_copy(
-            og_ref.at[:, cols], og_all.at[ch, :, cols], y_send.at[d - 1, p], y_recv.at[d - 1, p],
-            device_id={"ch": other}, device_id_type=MESH)
-
-    def fwd_copy(d, p):
-        cols = pl.ds(p * PIECE, PIECE)
-        owner = lax.rem(chip - d + n_chips, n_chips) * 2 + core
-        piece = og_all.at[owner, :, cols]
-        return pltpu.make_async_remote_copy(
-            piece, piece, fwd_send.at[d - 1, p], fwd_recv.at[d - 1, p],
-            device_id={"ch": sibling}, device_id_type=MESH)
-
-    core_copy = pltpu.make_async_remote_copy(
-        og_ref, og_all.at[ch], core_send, core_recv, device_id={"ch": sibling}, device_id_type=MESH)
-    for p in range(n_pieces):
-        for d in range(1, n_chips):
-            y_copy(d, p).start()
-    core_copy.start()
-
     inner_ext[tok:, :] = (k_ref[...].astype(F32) * v_ref[...].astype(F32)).astype(BF16)
-
-    def rim_copy():
-        return pltpu.make_async_remote_copy(
-            inner_ext.at[pl.ds(tok, tok)], inner_ext.at[pl.ds(0, tok)], rim_send, rim_recv,
-            device_id={"ctx": lax.rem(ctx + 1, n_ctx)}, device_id_type=MESH)
-
-    @pl.when(jnp.logical_not(last))
-    def _():
-        rim_copy().start()
-
     @pl.when(first)
     def _():
         inner_ext[:tok, :] = jnp.zeros((tok, chan), BF16)
@@ -117,6 +83,41 @@
     filt = f_ref[...]
     fl_ref[0] = filt.astype(F32)
     fl_ref[1] = jnp.dot(filt, negate, preferred_element_type=F32)
+    acc_ref[...] = jnp.zeros_like(acc_ref)
+
+    pl.semaphore_wait(barrier, len(offsets) + 1 + n_chips - 1)
+
+    def y_copy(d, p):
+        cols = pl.ds(p * PIECE, PIECE)
+        other = lax.rem(chip + d, n_chips) * 2 + core
+        return pltpu.make_async_remote_copy(
+            og_ref.at[:, cols], og_all.at[ch, :, cols], y_send.at[d - 1, p], y_recv.at[d - 1, p],
+            device_id={"ch": other}, device_id_type=MESH)
+
+    def fwd_copy(d, p):
+        cols = pl.ds(p * PIECE, PIECE)
+        owner = lax.rem(chip - d + n_chips, n_chips) * 2 + core
+        piece = og_all.at[owner, :, cols]
+        return pltpu.make_async_remote_copy(
+            piece, piece, fwd_send.at[d - 1, p], fwd_recv.at[d - 1, p],
+            device_id={"ch": sibling}, device_id_type=MESH)
+
+    core_copy = pltpu.make_async_remote_copy(
+        og_ref, og_all.at[ch], core_send, core_recv, device_id={"ch": sibling}, device_id_type=MESH)
+    for p in range(n_pieces):
+        for d in range(1, n_chips):
+            y_copy(d, p).start()
+    core_copy.start()
+
+
+    def rim_copy():
+        return pltpu.make_async_remote_copy(
+            inner_ext.at[pl.ds(tok, tok)], inner_ext.at[pl.ds(0, tok)], rim_send, rim_recv,
+            device_id={"ctx": lax.rem(ctx + 1, n_ctx)}, device_id_type=MESH)
+
+    @pl.when(jnp.logical_not(last))
+    def _():
+        rim_copy().start()
 
     def build(g, carry):
         rows = pl.ds(pl.multiple_of(g * tok, tok), tok)
@@ -145,7 +146,6 @@
     def multiply_block(index, owner):
         lax.fori_loop(0, n_pieces, lambda p, c: (multiply(index, owner, p), c)[1], 0)
 
-    acc_ref[...] = jnp.zeros_like(acc_ref)
     own_copy.wait()
     w_copy(0).wait()
     multiply_block(0, ch)

time: 42.6 us -> 42.6 us (level)
  no operation moved by 1% of the time
where the time goes in v3:
time: 42.6 us; the launch traced here: 42.5 us
  Pallas kernels  41.8 us (98%)
  between operations  0.64 us (2%)
    pallas_call x1, Pallas kernels, per_device(): pl.pallas_call(functools.partial(kernel_body, n_ctx, n_ch, reduce_here),...  39.6 us
    pallas_call x1, Pallas kernels, per_device(): pl.pallas_call(hand_on, out_shape=tuple((jax.ShapeDtypeStruct(x.shape, x....  2.21 us

profile of v3, /device:TPU:0, one launch (start us, length us, event | category | flops | bytes accessed | tf_op | source)
XLA Modules:
  0.0 42.5 jit_solution(16245485769173459499)
XLA Ops:
  0.6 39.6 %hyena.1 = (bf16[128,1024]{1,0:T(8,128)(2,1)}, bf16[128,1024]{1,0:T(8,128)(2,1)}, bf16[128,1024]{1,0:T(8,128)(2,1)}, bf16[128,1024]{1,0:T(8,128)(2,1)}, f32[8,8,128]{2,1,0:T(8,128)}, /*index=5*/f32[8,1,128]{2,1,0:T(1,128)}) custom-call(bf16[128,1024]{1,0:T(8,128)(2,1)} %refs_0_.1, bf16[128,1024]{1,0:T(8,128)(2,1)} %refs_1_.1, bf16[128,1024]{1,0:T(8,128)(2,1)} %refs_2_.1, ...), custom_call_target="tpu_custom_call" | custom-call | tf_op jit(solution)/shard_map/hyena/pallas_call | solution.py:344
  40.2 2.2 %hand_on.1 = (bf16[128,1024]{1,0:T(8,128)(2,1)}, bf16[128,1024]{1,0:T(8,128)(2,1)}, bf16[128,1024]{1,0:T(8,128)(2,1)}, bf16[128,1024]{1,0:T(8,128)(2,1)}, f32[8,8,128]{2,1,0:T(8,128)}, /*index=5*/f32[8,1,128]{2,1,0:T(1,128)}) custom-call(bf16[128,1024]{1,0:T(8,128)(2,1)} %get-tuple-element.18.refs_0_, bf16[128,1024]{1,0:T(8,128)(2,1)} %get-tuple-element.19.refs_1_, ...), custom_call_target="tpu_custom_call" | custom-call | tf_op jit(solution)/shard_map/hand_on/pallas_call | solution.py:381
